TPU v7x, 32 devices: a whole 2x2x4 slice. The times are simulated.
32 devices in a mesh: groups: 2 (over y), pipe: 4 (over z), hour: 2 (over x), seg: 2 (over core).
Axes of the slice: x: 2, y: 2, z: 4, core: 2. Of those that a mesh axis runs over, the one named last changes fastest.
Arguments:
- segment_flow: float32 [16, 64, 1024], P(('groups', 'hour'), 'seg', 'pipe'), parts along dimension 0, may hold values from -4 to 4
- linepack: float32 [16, 64, 1024], P(('groups', 'hour'), 'seg', 'pipe'), parts along dimension 0, may hold values from 0.2 to 2.4
- mass_dual: float32 [16, 64, 1024], P(('groups', 'hour'), 'seg', 'pipe'), parts along dimension 0, may hold values from -3 to 3
- momentum_dual: float32 [16, 64, 1024], P(('groups', 'hour'), 'seg', 'pipe'), parts along dimension 0, may hold values from -3 to 3
- contract_dual: float32 [16, 2, 32, 128], P(('groups', 'hour'), 'seg', 'pipe'), parts along dimension 0, may hold values from -3 to 3
- flow_cost: float32 [16, 64, 1024], P(('groups', 'hour'), 'seg', 'pipe'), parts along dimension 0, may hold values from -24 to 24
- injection: float32 [16, 64, 1024], P(('groups', 'hour'), 'seg', 'pipe'), parts along dimension 0, may hold values from -3 to 3
- contract_target: float32 [16, 2, 32, 128], P(('groups', 'hour'), 'seg', 'pipe'), parts along dimension 0, may hold values from 0.4 to 2
- friction_table: float32 [16], replicated, may hold values from 0.3 to 3
- friction_class: int32 [64, 2048], P('seg', ('groups', 'pipe')), parts along dimension 1, may hold values from 0 to 15
- matching: int32 [2048], P('groups'), parts along dimension 0, may hold values from 0 to 1023, as said below
- contract_map: int32 [16, 1024], P(('groups', 'hour')), parts along dimension 0, may hold values from 0 to 127
Outputs:
- flow_final: float32 [16, 64, 1024], P(('groups', 'hour'), 'seg', 'pipe'), parts along dimension 0
- linepack_final: float32 [16, 64, 1024], P(('groups', 'hour'), 'seg', 'pipe'), parts along dimension 0
- mass_dual_final: float32 [16, 64, 1024], P(('groups', 'hour'), 'seg', 'pipe'), parts along dimension 0
- momentum_dual_final: float32 [16, 64, 1024], P(('groups', 'hour'), 'seg', 'pipe'), parts along dimension 0
- contract_dual_final: float32 [16, 2, 32, 128], P(('groups', 'hour'), 'seg', 'pipe'), parts along dimension 0
- primal_weight: float32 [2], P('groups'), parts along dimension 0
There are 2 independent parts, one for each index of `groups`. A program takes and returns all parts, laid end to end along the dimension named above; an argument that names none is the same for every part. Nothing has to cross between parts.
Inputs may be any that keep to these rules, and one draw needn't show every extreme that they name: `matching`: every pipe's inlet is fed by the outlet of exactly one pipe: each number of 0 to 1023 appears once; for any two blocks of 256 consecutive pipes, exactly 64 pipes of the first are fed from outlets of the second.
All inputs are finite; a program needn't handle non-finite values.
Results may differ from a plain program's by a relative error of at most 0.0001.
Values sent between devices are 32-bit elements; how exact they have to be, the bound alone decides.
A program may use at most 64 MiB of HBM per device.

v0:
```python
import math
import jax
import jax.numpy as jnp
from jax import lax
from jax.sharding import PartitionSpec as P

ITERS = 2
FLOW_CAP = 1.5
PACK_CAP = 2.5
STEP_SCALE = 0.25
NORM_EPS = 1e-06


def padded(cells, sides, width):
    for axis, dim in sides:
        count = lax.axis_size(axis)
        ends = count - 1
        head = lax.slice_in_dim(cells, 0, width, axis=dim)
        tail = lax.slice_in_dim(cells, cells.shape[dim] - width, cells.shape[dim], axis=dim)
        cells = jnp.concatenate(
            [
                lax.ppermute(tail, axis, [(i, (i + 1) % count) for i in range(ends)]),
                cells,
                lax.ppermute(head, axis, [((i + 1) % count, i) for i in range(ends)]),
            ],
            axis=dim,
        )
    return cells


def widened_pair(stacked):
    return padded(stacked, (("hour", 1), ("seg", 2)), 1)


def other_half(edge_row, half_index, partner_local):
    gathered = lax.all_gather(edge_row[:, None, :], ("pipe", "seg"), axis=1, tiled=True)
    hour_rows, row_count, row_width = gathered.shape
    seg_count = lax.axis_size("seg")
    picked = gathered.reshape(hour_rows, row_count // seg_count, seg_count, row_width)[
        :, :, half_index, :
    ]
    far_rows = picked.reshape(hour_rows, row_count // seg_count * row_width)
    return jnp.take(far_rows, partner_local, axis=1)


def contract_local(values, contract_rows, class_count):
    hour_rows, seg_rows, pipe_rows = values.shape
    block = math.gcd(pipe_rows, 2048)
    classes = jnp.arange(class_count, dtype=jnp.int32)

    def add_block(block_index, total):
        partial_value = lax.dynamic_slice_in_dim(values, block_index * block, block, 2)
        row_map = lax.dynamic_slice_in_dim(contract_rows, block_index * block, block, 1)
        onehot = (row_map[:, :, None] == classes[None, None, :]).astype(jnp.float32)
        return total + jnp.einsum(
            "hsp,hpc->hsc",
            partial_value,
            onehot,
            precision=lax.Precision.HIGHEST,
            preferred_element_type=jnp.float32,
        )

    return lax.fori_loop(
        0, pipe_rows // block, add_block, jnp.zeros((hour_rows, seg_rows, class_count), jnp.float32)
    )


def spread_local(duals, contract_rows):
    hour_rows, seg_rows, class_count = duals.shape
    pipe_rows = contract_rows.shape[1]
    block = math.gcd(pipe_rows, 2048)
    classes = jnp.arange(class_count, dtype=jnp.int32)

    def fill_block(block_index, result_now):
        row_map = lax.dynamic_slice_in_dim(contract_rows, block_index * block, block, 1)
        onehot = (row_map[:, :, None] == classes[None, None, :]).astype(jnp.float32)
        partial_value = jnp.einsum(
            "hsc,hpc->hsp",
            duals,
            onehot,
            precision=lax.Precision.HIGHEST,
            preferred_element_type=jnp.float32,
        )
        return lax.dynamic_update_slice_in_dim(result_now, partial_value, block_index * block, 2)

    return lax.fori_loop(
        0, pipe_rows // block, fill_block, jnp.zeros((hour_rows, seg_rows, pipe_rows), jnp.float32)
    )


def on_device(
    segment_flow,
    linepack,
    mass_dual,
    momentum_dual,
    contract_dual,
    flow_cost,
    injection,
    contract_target,
    friction_table,
    friction_class,
    matching,
    contract_map,
):
    hour_rows, seg_rows, pipe_rows = segment_flow.shape
    class_count = contract_dual.shape[3]
    pipe_count = lax.axis_size("pipe")
    total_pipes = pipe_rows * pipe_count
    share_scale = class_count / total_pipes
    pipe_start = lax.axis_index("pipe") * pipe_rows
    seg_index = lax.axis_index("seg")
    at_start = seg_index == 0
    at_end = seg_index == lax.axis_size("seg") - 1
    levels = jnp.arange(friction_table.shape[0], dtype=jnp.int32)
    friction = jnp.sum(
        jnp.where(
            friction_class[None] == levels[:, None, None], friction_table[:, None, None], 0.0
        ),
        axis=0,
    )[None]
    inverse = (
        jnp.zeros_like(matching).at[matching].set(jnp.arange(matching.shape[0], dtype=jnp.int32))
    )
    source_local = lax.dynamic_slice_in_dim(matching, pipe_start, pipe_rows)
    target_local = lax.dynamic_slice_in_dim(inverse, pipe_start, pipe_rows)
    contract_now = contract_dual.reshape(hour_rows, contract_dual.shape[2], class_count)
    target_now = contract_target.reshape(hour_rows, contract_target.shape[2], class_count)
    weight = jnp.float32(1.0)
    for iteration in range(ITERS):
        primal_step = STEP_SCALE / weight
        dual_step = STEP_SCALE * weight
        widened = widened_pair(jnp.stack([mass_dual, momentum_dual]))
        last_base = widened[0, 1:-1, -1, :]
        later_hour = widened[0, 2:, 1:-1, :]
        before_seg = widened[1, 1:-1, :-2, :]
        returned = other_half(mass_dual[:, 0, :], 0, target_local)
        last_row = last_base + jnp.where(at_end, returned, 0.0)
        next_seg = jnp.concatenate([mass_dual[:, 1:, :], last_row[:, None, :]], axis=1)
        grad_flow = mass_dual - next_seg + friction * momentum_dual
        hour_spread = spread_local(contract_now, contract_map)
        spread = lax.all_to_all(hour_spread, "pipe", split_axis=2, concat_axis=1, tiled=True)
        grad_pack = mass_dual - later_hour - momentum_dual + before_seg + share_scale * spread
        grad_flow, grad_pack = (grad_flow, grad_pack)
        flow_next = jnp.clip(
            segment_flow - primal_step * (flow_cost - grad_flow), -FLOW_CAP, FLOW_CAP
        )
        pack_next = jnp.clip(linepack + primal_step * grad_pack, 0.0, PACK_CAP)
        flow_bar = 2.0 * flow_next - segment_flow
        pack_bar = 2.0 * pack_next - linepack
        forward_widened = widened_pair(jnp.stack([flow_bar, pack_bar]))
        first_base = forward_widened[0, 1:-1, 0, :]
        earlier = forward_widened[1, :-2, 1:-1, :]
        after_seg = forward_widened[1, 1:-1, 2:, :]
        inflow = other_half(flow_bar[:, -1, :], 1, source_local)
        first_row = first_base + jnp.where(at_start, inflow, 0.0)
        upstream = jnp.concatenate([first_row[:, None, :], flow_bar[:, :-1, :]], axis=1)
        mass_rows = pack_bar - earlier + flow_bar - upstream
        momentum = friction * flow_bar - (pack_bar - after_seg)
        hour_major = lax.all_to_all(pack_bar, "pipe", split_axis=1, concat_axis=2, tiled=True)
        totals = contract_local(hour_major, contract_map, class_count)
        mass_rows, momentum, totals = (mass_rows, momentum, share_scale * totals)
        mass_next = mass_dual + dual_step * (injection - mass_rows)
        momentum_next = momentum_dual - dual_step * momentum
        contract_next = contract_now + dual_step * (target_now - totals)
        primal_sq = jnp.sum((flow_next - segment_flow) ** 2) + jnp.sum((pack_next - linepack) ** 2)
        dual_sq = (
            jnp.sum((mass_next - mass_dual) ** 2)
            + jnp.sum((momentum_next - momentum_dual) ** 2)
            + jnp.sum((contract_next - contract_now) ** 2)
        )
        primal_total, dual_total = lax.psum((primal_sq, dual_sq), ("pipe", "hour", "seg"))
        weight = jnp.sqrt(weight * jnp.sqrt((dual_total + NORM_EPS) / (primal_total + NORM_EPS)))
        segment_flow, linepack = (flow_next, pack_next)
        mass_dual, momentum_dual, contract_now = (mass_next, momentum_next, contract_next)
    return (
        segment_flow,
        linepack,
        mass_dual,
        momentum_dual,
        contract_now.reshape(contract_dual.shape),
        weight.reshape(1),
    )


def solution(mesh):
    return jax.shard_map(
        on_device,
        mesh=mesh,
        in_specs=(
            P(("groups", "hour"), "seg", "pipe"),
            P(("groups", "hour"), "seg", "pipe"),
            P(("groups", "hour"), "seg", "pipe"),
            P(("groups", "hour"), "seg", "pipe"),
            P(("groups", "hour"), "seg", "pipe", None),
            P(("groups", "hour"), "seg", "pipe"),
            P(("groups", "hour"), "seg", "pipe"),
            P(("groups", "hour"), "seg", "pipe", None),
            P(),
            P("seg", ("groups", "pipe")),
            P("groups"),
            P(("groups", "hour"), None),
        ),
        out_specs=(
            P(("groups", "hour"), "seg", "pipe"),
            P(("groups", "hour"), "seg", "pipe"),
            P(("groups", "hour"), "seg", "pipe"),
            P(("groups", "hour"), "seg", "pipe"),
            P(("groups", "hour"), "seg", "pipe", None),
            P("groups"),
        ),
        check_vma=False,
    )
```

profile of v0, /device:TPU:0, one launch (start us, length us, event | category | flops | bytes accessed | tf_op | source)
XLA Modules:
  0.0 255.9 jit_solution(9958504613072737630)
XLA Ops:
  0.6 2.2 fusion.4
  2.9 0.8 copy.144
  3.7 3.1 %reshape.116 = f32[4,1,8192]{2,1,0:T(1,128)} reshape(f32[1024,4,8]{2,1,0:T(4,128)S(1)} %bitcast.195) | data formatting | bytes 262144
  6.8 6.3 %all-to-all-start = ((f32[4,1,8192]{2,1,0:T(1,128)}), f32[4,1,8192]{2,1,0:T(1,128)S(1)}, u32[]{:S(2)}, u32[]{:S(2)}) async-start(f32[4,1,8192]{2,1,0:T(1,128)} %reshape.116), calls=%async_computation | async-start | bytes 262144 | tf_op jit(solution)/shard_map/all_to_all | solution.py:141
  13.2 1.3 collective-permute-start.1
  14.5 4.5 %collective-permute-start = (f32[2,1,32,256]{3,2,1,0:T(8,128)S(1)}, f32[2,1,32,256]{3,2,1,0:T(8,128)S(1)}, u32[]{:S(2)}, u32[]{:S(2)}) collective-permute-start(f32[2,1,32,256]{3,2,1,0:T(8,128)S(1)} %get-tuple-element.135), channel_id=1, source_target_pairs={{0,2},{1,3},{4,6},{5,7},{8,10},{9,11},{12,14},{13,15},{16,18},{17,... | collective-permute-start | bytes 196616 | tf_op jit(solution)/shard_map/ppermute | solution.py:22
  19.1 14.6 %all_gather.12 = f32[4,8,256]{2,0,1:T(4,128)S(1)} all-gather(f32[4,1,256]{2,0,1:T(4,128)S(1)} %copy.255), channel_id=1, replica_groups=mesh['groups'=2,'pipe'=4,'hour'=2,'seg'=2] {'pipe','seg'}, dimensions={1}, use_global_device_ids=true | all-gather | bytes 36864 | tf_op jit(solution)/shard_map/all_gather | solution.py:36
  33.9 4.3 %scatter_custom_fusion = s32[1024]{0:T(1024)S(1)} fusion(s32[1024]{0:T(1024)S(1)} %compare_select_fusion, s32[1024]{0:T(1024)S(1)} %iota.14, s32[]{:T(128)} %constant.26.clone.1), kind=kCustom, calls=%fused_computation.140 | custom fusion | bytes 4100 | tf_op jit(solution)/shard_map/scatter | solution.py:122
  38.3 0.7 copy.256
  39.2 0.7 gather_fusion
  40.3 2.2 collective-permute-start.3
  42.7 1.3 collective-permute-start.2
  44.6 1.5 collective-permute-done.2
  46.8 1.0 reduce
  47.8 2.5 reshape.117
  50.4 1.8 broadcast_multiply_fusion.1
  52.2 1.9 copy.145
  54.1 1.2 multiply_reduce_fusion.4
  55.4 0.8 multiply_subtract_fusion.3
  56.3 0.9 copy_dynamic-update-slice_fusion.4
  57.2 1.4 collective-permute-start.5
  58.7 4.5 %collective-permute-start.4 = (f32[2,1,32,256]{3,2,1,0:T(8,128)S(1)}, f32[2,1,32,256]{3,2,1,0:T(8,128)S(1)}, u32[]{:S(2)}, u32[]{:S(2)}) collective-permute-start(f32[2,1,32,256]{3,2,1,0:T(8,128)S(1)} %get-tuple-element.131), channel_id=1, source_target_pairs={{0,2},{1,3},{4,6},{5,7},{8,10},{9,11},{12,14},{13,15},{16,18},{17,... | collective-permute-start | bytes 196616 | tf_op jit(solution)/shard_map/ppermute | solution.py:22
  63.3 14.0 %all_gather.13 = f32[4,8,256]{2,0,1:T(4,128)S(1)} all-gather(f32[4,1,256]{2,0,1:T(4,128)S(1)} %slice.182), channel_id=1, replica_groups=mesh['groups'=2,'pipe'=4,'hour'=2,'seg'=2] {'pipe','seg'}, dimensions={1}, use_global_device_ids=true | all-gather | bytes 36864 | tf_op jit(solution)/shard_map/all_gather | solution.py:36
  77.5 0.7 gather_fusion.1
  78.7 2.2 collective-permute-start.6
  81.0 1.5 collective-permute-start.7
  82.7 1.4 collective-permute-done.7
  84.0 2.0 multiply_reduce_fusion.7
  86.2 1.3 collective-permute-start.9
  87.5 4.5 %collective-permute-start.8 = (f32[2,1,32,256]{3,2,1,0:T(8,128)S(1)}, f32[2,1,32,256]{3,2,1,0:T(8,128)S(1)}, u32[]{:S(2)}, u32[]{:S(2)}) collective-permute-start(f32[2,1,32,256]{3,2,1,0:T(8,128)S(1)} %get-tuple-element.127), channel_id=1, source_target_pairs={{0,2},{1,3},{4,6},{5,7},{8,10},{9,11},{12,14},{13,15},{16,18},{17,... | collective-permute-start | bytes 196616 | tf_op jit(solution)/shard_map/ppermute | solution.py:22
  92.0 4.5 %all-to-all-start.1 = ((f32[4,32,256]{2,0,1:T(4,128)}), f32[4,32,256]{2,0,1:T(4,128)S(1)}, u32[]{:S(2)}, u32[]{:S(2)}) async-start(f32[4,32,256]{2,0,1:T(4,128)} %multiply_subtract_fusion.3), calls=%async_computation.1 | async-start | bytes 262144 | tf_op jit(solution)/shard_map/all_to_all | solution.py:159
  98.5 14.6 %all_gather.14 = f32[4,8,256]{2,0,1:T(4,128)S(1)} all-gather(f32[4,1,256]{2,0,1:T(4,128)S(1)} %slice.191), channel_id=1, replica_groups=mesh['groups'=2,'pipe'=4,'hour'=2,'seg'=2] {'pipe','seg'}, dimensions={1}, use_global_device_ids=true | all-gather | bytes 36864 | tf_op jit(solution)/shard_map/all_gather | solution.py:36
  113.3 1.3 gather_fusion.2
  116.3 2.2 collective-permute-start.11
  118.5 0.9 copy.197
  119.3 1.3 collective-permute-start.10
  120.7 2.2 fusion.73
  122.9 1.8 fusion.1
  124.8 0.8 copy.174
  125.6 3.1 %reshape.118 = f32[4,1,8192]{2,1,0:T(1,128)} reshape(f32[1024,4,8]{2,1,0:T(4,128)S(1)} %bitcast.197) | data formatting | bytes 262144
  128.7 4.5 %all-to-all-start.2 = ((f32[4,1,8192]{2,1,0:T(1,128)}), f32[4,1,8192]{2,1,0:T(1,128)S(1)}, u32[]{:S(2)}, u32[]{:S(2)}) async-start(f32[4,1,8192]{2,1,0:T(1,128)} %reshape.118), calls=%async_computation.2 | async-start | bytes 262144 | tf_op jit(solution)/shard_map/all_to_all | solution.py:141
  133.2 1.1 fusion.31
  135.1 33.5 %all-reduce.1 = (f32[]{:T(128)}, f32[]{:T(128)}) all-reduce(f32[]{:T(128)S(6)} %add.153, f32[]{:T(128)S(6)} %add.155), channel_id=1, replica_groups=mesh['groups'=2,'pipe'=4,'hour'=2,'seg'=2] {'pipe','hour','seg'}, use_global_device_ids=true, to_apply=%region_5.7 | all-reduce | flops 2 | bytes 16 | tf_op jit(solution)/shard_map/psum | solution.py:171
  170.1 1.0 reduce.1
  171.0 2.5 reshape.119
  173.6 1.8 broadcast_multiply_fusion
  175.4 1.9 copy.175
  177.3 0.9 multiply_reduce_fusion
  178.2 0.7 multiply_subtract_fusion.1
  179.0 0.9 copy_dynamic-update-slice_fusion
  180.0 1.3 collective-permute-start.13
  181.3 4.5 %collective-permute-start.12 = (f32[2,1,32,256]{3,2,1,0:T(8,128)S(1)}, f32[2,1,32,256]{3,2,1,0:T(8,128)S(1)}, u32[]{:S(2)}, u32[]{:S(2)}) collective-permute-start(f32[2,1,32,256]{3,2,1,0:T(8,128)S(1)} %get-tuple-element.123), channel_id=1, source_target_pairs={{0,2},{1,3},{4,6},{5,7},{8,10},{9,11},{12,14},{13,15},{16,18},{17,... | collective-permute-start | bytes 196616 | tf_op jit(solution)/shard_map/ppermute | solution.py:22
  185.8 0.7 copy.186
  186.5 0.7 copy.187
  187.2 3.5 %all-to-all-start.3 = ((f32[4,32,256]{2,0,1:T(4,128)}), f32[4,32,256]{2,0,1:T(4,128)S(1)}, u32[]{:S(2)}, u32[]{:S(2)}) async-start(f32[4,32,256]{2,0,1:T(4,128)} %multiply_subtract_fusion.1), calls=%async_computation.3 | async-start | bytes 262144 | tf_op jit(solution)/shard_map/all_to_all | solution.py:159
  190.7 14.6 %all_gather.15 = f32[4,8,256]{2,0,1:T(4,128)S(1)} all-gather(f32[4,1,256]{2,0,1:T(4,128)S(1)} %slice.198), channel_id=1, replica_groups=mesh['groups'=2,'pipe'=4,'hour'=2,'seg'=2] {'pipe','seg'}, dimensions={1}, use_global_device_ids=true | all-gather | bytes 36864 | tf_op jit(solution)/shard_map/all_gather | solution.py:36
  205.6 0.7 gather_fusion.3
  207.9 1.3 collective-permute-start.15
  209.4 3.0 %collective-permute-start.14 = (f32[2,6,1,256]{1,3,2,0:T(8,128)S(1)}, f32[2,6,1,256]{1,3,2,0:T(8,128)S(1)}, u32[]{:S(2)}, u32[]{:S(2)}) collective-permute-start(f32[2,6,1,256]{1,3,2,0:T(8,128)S(1)} %copy.201), channel_id=1, source_target_pairs={{0,1},{2,3},{4,5},{6,7},{8,9},{10,11},{12,13},{14,15},{16,17},{18,... | collective-permute-start | bytes 36872 | tf_op jit(solution)/shard_map/ppermute | solution.py:22
  212.4 1.1 collective-permute-done.14
  213.8 1.8 multiply_reduce_fusion.2
  217.6 2.4 multiply_reduce_fusion.8
  220.7 0.7 copy.189
  221.4 32.0 %all-reduce = (f32[]{:T(128)}, f32[]{:T(128)}) all-reduce(f32[]{:T(128)S(6)} %add.167, f32[]{:T(128)S(6)} %add.169), channel_id=1, replica_groups=mesh['groups'=2,'pipe'=4,'hour'=2,'seg'=2] {'pipe','hour','seg'}, use_global_device_ids=true, to_apply=%region_12.14 | all-reduce | flops 2 | bytes 16 | tf_op jit(solution)/shard_map/psum | solution.py:171
  (119 shorter events, 6.6 us)
Async XLA Ops:
  2.8 10.3 %copy-start = (f32[4,32,256]{2,1,0:T(8,128)S(1)}, f32[4,32,256]{2,1,0:T(8,128)}, u32[]{:S(2)}) copy-start(f32[4,32,256]{2,1,0:T(8,128)} %param.16) | copy-start | bytes 393220
  2.8 10.3 %copy-start.1 = (f32[4,32,256]{2,1,0:T(8,128)S(1)}, f32[4,32,256]{2,1,0:T(8,128)}, u32[]{:S(2)}) copy-start(f32[4,32,256]{2,1,0:T(8,128)} %param.17) | copy-start | bytes 393220
  3.7 30.2 %copy-start.12 = (s32[1024]{0:T(1024)S(1)}, s32[1024]{0:T(1024)}, u32[]{:S(2)}) copy-start(s32[1024]{0:T(1024)} %param.24) | copy-start | bytes 12292
  3.7 35.3 %copy-start.11 = (s32[32,256]{1,0:T(8,128)S(1)}, s32[32,256]{1,0:T(8,128)}, u32[]{:S(2)}) copy-start(s32[32,256]{1,0:T(8,128)} %param.23) | copy-start | bytes 98308
  3.7 35.3 %copy-start.13 = (f32[16]{0:T(128)S(1)}, f32[16]{0:T(128)}, u32[]{:S(2)}) copy-start(f32[16]{0:T(128)} %param.22) | copy-start | bytes 196
  6.8 39.5 %all-to-all-start = ((f32[4,1,8192]{2,1,0:T(1,128)}), f32[4,1,8192]{2,1,0:T(1,128)S(1)}, u32[]{:S(2)}, u32[]{:S(2)}) async-start(f32[4,1,8192]{2,1,0:T(1,128)} %reshape.116), calls=%async_computation | async-start | bytes 262144 | tf_op jit(solution)/shard_map/all_to_all | solution.py:141
  13.2 26.8 %collective-permute-start.1 = (f32[2,1,32,256]{3,2,1,0:T(8,128)S(1)}, f32[2,1,32,256]{3,2,1,0:T(8,128)S(1)}, u32[]{:S(2)}, u32[]{:S(2)}) collective-permute-start(f32[2,1,32,256]{3,2,1,0:T(8,128)S(1)} %get-tuple-element.136), channel_id=1, source_target_pairs={{2,0},{3,1},{6,4},{7,5},{10,8},{11,9},{14,12},{15,13},{18,16},{19,... | collective-permute-start | bytes 196616 | tf_op jit(solution)/shard_map/ppermute | solution.py:24
  14.5 25.5 %collective-permute-start = (f32[2,1,32,256]{3,2,1,0:T(8,128)S(1)}, f32[2,1,32,256]{3,2,1,0:T(8,128)S(1)}, u32[]{:S(2)}, u32[]{:S(2)}) collective-permute-start(f32[2,1,32,256]{3,2,1,0:T(8,128)S(1)} %get-tuple-element.135), channel_id=1, source_target_pairs={{0,2},{1,3},{4,6},{5,7},{8,10},{9,11},{12,14},{13,15},{16,18},{17,... | collective-permute-start | bytes 196616 | tf_op jit(solution)/shard_map/ppermute | solution.py:22
  40.3 13.8 %collective-permute-start.3 = (f32[2,6,1,256]{3,1,2,0:T(8,128)S(1)}, f32[2,6,1,256]{3,1,2,0:T(8,128)S(1)}, u32[]{:S(2)}, u32[]{:S(2)}) collective-permute-start(f32[2,6,1,256]{3,1,2,0:T(8,128)S(1)} %slice.177), channel_id=1, source_target_pairs={{0,1},{2,3},{4,5},{6,7},{8,9},{10,11},{12,13},{14,15},{16,17},{18,... | collective-permute-start | bytes 36872 | tf_op jit(solution)/shard_map/ppermute | solution.py:22
  42.7 3.4 %collective-permute-start.2 = (f32[2,6,1,256]{1,3,2,0:T(8,128)S(1)}, f32[2,6,1,256]{1,3,2,0:T(8,128)S(1)}, u32[]{:S(2)}, u32[]{:S(2)}) collective-permute-start(f32[2,6,1,256]{1,3,2,0:T(8,128)S(1)} %copy.191), channel_id=1, source_target_pairs={{1,0},{3,2},{5,4},{7,6},{9,8},{11,10},{13,12},{15,14},{17,16},{19,... | collective-permute-start | bytes 36872 | tf_op jit(solution)/shard_map/ppermute | solution.py:24
  52.1 1.9 copy-start.2
  52.2 2.0 copy-start.3
  52.2 2.0 copy-start.4
  52.2 2.0 copy-start.8
  52.2 2.0 copy-start.9
  57.2 26.8 %copy-start.6 = (f32[4,32,256]{2,1,0:T(8,128)S(1)}, f32[4,32,256]{2,1,0:T(8,128)}, u32[]{:S(2)}) copy-start(f32[4,32,256]{2,1,0:T(8,128)} %param.20) | copy-start | bytes 393220
  57.2 21.0 %collective-permute-start.5 = (f32[2,1,32,256]{3,2,1,0:T(8,128)S(1)}, f32[2,1,32,256]{3,2,1,0:T(8,128)S(1)}, u32[]{:S(2)}, u32[]{:S(2)}) collective-permute-start(f32[2,1,32,256]{3,2,1,0:T(8,128)S(1)} %get-tuple-element.132), channel_id=1, source_target_pairs={{2,0},{3,1},{6,4},{7,5},{10,8},{11,9},{14,12},{15,13},{18,16},{19,... | collective-permute-start | bytes 196616 | tf_op jit(solution)/shard_map/ppermute | solution.py:24
  58.7 19.6 %collective-permute-start.4 = (f32[2,1,32,256]{3,2,1,0:T(8,128)S(1)}, f32[2,1,32,256]{3,2,1,0:T(8,128)S(1)}, u32[]{:S(2)}, u32[]{:S(2)}) collective-permute-start(f32[2,1,32,256]{3,2,1,0:T(8,128)S(1)} %get-tuple-element.131), channel_id=1, source_target_pairs={{0,2},{1,3},{4,6},{5,7},{8,10},{9,11},{12,14},{13,15},{16,18},{17,... | collective-permute-start | bytes 196616 | tf_op jit(solution)/shard_map/ppermute | solution.py:22
  78.7 3.7 %collective-permute-start.6 = (f32[2,6,1,256]{1,3,2,0:T(8,128)S(1)}, f32[2,6,1,256]{1,3,2,0:T(8,128)S(1)}, u32[]{:S(2)}, u32[]{:S(2)}) collective-permute-start(f32[2,6,1,256]{1,3,2,0:T(8,128)S(1)} %copy.195), channel_id=1, source_target_pairs={{0,1},{2,3},{4,5},{6,7},{8,9},{10,11},{12,13},{14,15},{16,17},{18,... | collective-permute-start | bytes 36872 | tf_op jit(solution)/shard_map/ppermute | solution.py:22
  81.0 3.1 %collective-permute-start.7 = (f32[2,6,1,256]{3,1,2,0:T(8,128)S(1)}, f32[2,6,1,256]{3,1,2,0:T(8,128)S(1)}, u32[]{:S(2)}, u32[]{:S(2)}) collective-permute-start(f32[2,6,1,256]{3,1,2,0:T(8,128)S(1)} %slice.185), channel_id=1, source_target_pairs={{1,0},{3,2},{5,4},{7,6},{9,8},{11,10},{13,12},{15,14},{17,16},{19,... | collective-permute-start | bytes 36872 | tf_op jit(solution)/shard_map/ppermute | solution.py:24
  86.1 34.6 %copy-start.14 = (f32[4,1,8,128]{3,2,1,0:T(8,128)S(1)}, f32[4,1,8,128]{3,2,1,0:T(8,128)}, u32[]{:S(2)}) copy-start(f32[4,1,8,128]{3,2,1,0:T(8,128)} %param.18) | copy-start | bytes 49156
  86.1 34.6 %copy-start.15 = (s32[4,1024]{1,0:T(4,128)S(1)}, s32[4,1024]{1,0:T(4,128)}, u32[]{:S(2)}) copy-start(s32[4,1024]{1,0:T(4,128)} %param.25) | copy-start | bytes 49156
  86.1 34.6 %copy-start.16 = (f32[4,1,8,128]{3,2,1,0:T(8,128)S(1)}, f32[4,1,8,128]{3,2,1,0:T(8,128)}, u32[]{:S(2)}) copy-start(f32[4,1,8,128]{3,2,1,0:T(8,128)} %param.21) | copy-start | bytes 49156
  86.2 29.8 %collective-permute-start.9 = (f32[2,1,32,256]{3,2,1,0:T(8,128)S(1)}, f32[2,1,32,256]{3,2,1,0:T(8,128)S(1)}, u32[]{:S(2)}, u32[]{:S(2)}) collective-permute-start(f32[2,1,32,256]{3,2,1,0:T(8,128)S(1)} %get-tuple-element.128), channel_id=1, source_target_pairs={{2,0},{3,1},{6,4},{7,5},{10,8},{11,9},{14,12},{15,13},{18,16},{19,... | collective-permute-start | bytes 196616 | tf_op jit(solution)/shard_map/ppermute | solution.py:24
  87.5 28.5 %collective-permute-start.8 = (f32[2,1,32,256]{3,2,1,0:T(8,128)S(1)}, f32[2,1,32,256]{3,2,1,0:T(8,128)S(1)}, u32[]{:S(2)}, u32[]{:S(2)}) collective-permute-start(f32[2,1,32,256]{3,2,1,0:T(8,128)S(1)} %get-tuple-element.127), channel_id=1, source_target_pairs={{0,2},{1,3},{4,6},{5,7},{8,10},{9,11},{12,14},{13,15},{16,18},{17,... | collective-permute-start | bytes 196616 | tf_op jit(solution)/shard_map/ppermute | solution.py:22
  92.0 28.6 %all-to-all-start.1 = ((f32[4,32,256]{2,0,1:T(4,128)}), f32[4,32,256]{2,0,1:T(4,128)S(1)}, u32[]{:S(2)}, u32[]{:S(2)}) async-start(f32[4,32,256]{2,0,1:T(4,128)} %multiply_subtract_fusion.3), calls=%async_computation.1 | async-start | bytes 262144 | tf_op jit(solution)/shard_map/all_to_all | solution.py:159
  116.3 61.0 %collective-permute-start.11 = (f32[2,6,1,256]{3,1,2,0:T(8,128)S(1)}, f32[2,6,1,256]{3,1,2,0:T(8,128)S(1)}, u32[]{:S(2)}, u32[]{:S(2)}) collective-permute-start(f32[2,6,1,256]{3,1,2,0:T(8,128)S(1)} %slice.193), channel_id=1, source_target_pairs={{0,1},{2,3},{4,5},{6,7},{8,9},{10,11},{12,13},{14,15},{16,17},{18,... | collective-permute-start | bytes 36872 | tf_op jit(solution)/shard_map/ppermute | solution.py:22
  119.3 13.9 %collective-permute-start.10 = (f32[2,6,1,256]{1,3,2,0:T(8,128)}, f32[2,6,1,256]{1,3,2,0:T(8,128)}, u32[]{:S(2)}, u32[]{:S(2)}) collective-permute-start(f32[2,6,1,256]{1,3,2,0:T(8,128)} %copy.197), channel_id=1, source_target_pairs={{1,0},{3,2},{5,4},{7,6},{9,8},{11,10},{13,12},{15,14},{17,16},{19,... | collective-permute-start | bytes 36872 | tf_op jit(solution)/shard_map/ppermute | solution.py:24
  128.7 41.3 %all-to-all-start.2 = ((f32[4,1,8192]{2,1,0:T(1,128)}), f32[4,1,8192]{2,1,0:T(1,128)S(1)}, u32[]{:S(2)}, u32[]{:S(2)}) async-start(f32[4,1,8192]{2,1,0:T(1,128)} %reshape.118), calls=%async_computation.2 | async-start | bytes 262144 | tf_op jit(solution)/shard_map/all_to_all | solution.py:141
  175.4 1.9 copy-start.5
  175.4 1.9 copy-start.10
  180.0 27.6 %collective-permute-start.13 = (f32[2,1,32,256]{3,2,1,0:T(8,128)S(1)}, f32[2,1,32,256]{3,2,1,0:T(8,128)S(1)}, u32[]{:S(2)}, u32[]{:S(2)}) collective-permute-start(f32[2,1,32,256]{3,2,1,0:T(8,128)S(1)} %get-tuple-element.124), channel_id=1, source_target_pairs={{2,0},{3,1},{6,4},{7,5},{10,8},{11,9},{14,12},{15,13},{18,16},{19,... | collective-permute-start | bytes 196616 | tf_op jit(solution)/shard_map/ppermute | solution.py:24
  181.3 26.3 %collective-permute-start.12 = (f32[2,1,32,256]{3,2,1,0:T(8,128)S(1)}, f32[2,1,32,256]{3,2,1,0:T(8,128)S(1)}, u32[]{:S(2)}, u32[]{:S(2)}) collective-permute-start(f32[2,1,32,256]{3,2,1,0:T(8,128)S(1)} %get-tuple-element.123), channel_id=1, source_target_pairs={{0,2},{1,3},{4,6},{5,7},{8,10},{9,11},{12,14},{13,15},{16,18},{17,... | collective-permute-start | bytes 196616 | tf_op jit(solution)/shard_map/ppermute | solution.py:22
  187.2 26.6 %copy-start.7 = (f32[4,32,256]{2,1,0:T(8,128)S(1)}, f32[4,32,256]{2,1,0:T(8,128)}, u32[]{:S(2)}) copy-start(f32[4,32,256]{2,1,0:T(8,128)} %param.20) | copy-start | bytes 393220
  187.2 30.4 %all-to-all-start.3 = ((f32[4,32,256]{2,0,1:T(4,128)}), f32[4,32,256]{2,0,1:T(4,128)S(1)}, u32[]{:S(2)}, u32[]{:S(2)}) async-start(f32[4,32,256]{2,0,1:T(4,128)} %multiply_subtract_fusion.1), calls=%async_computation.3 | async-start | bytes 262144 | tf_op jit(solution)/shard_map/all_to_all | solution.py:159
  207.9 5.8 %collective-permute-start.15 = (f32[2,6,1,256]{3,1,2,0:T(8,128)S(1)}, f32[2,6,1,256]{3,1,2,0:T(8,128)S(1)}, u32[]{:S(2)}, u32[]{:S(2)}) collective-permute-start(f32[2,6,1,256]{3,1,2,0:T(8,128)S(1)} %slice.201), channel_id=1, source_target_pairs={{1,0},{3,2},{5,4},{7,6},{9,8},{11,10},{13,12},{15,14},{17,16},{19,... | collective-permute-start | bytes 36872 | tf_op jit(solution)/shard_map/ppermute | solution.py:24
  209.4 4.2 %collective-permute-start.14 = (f32[2,6,1,256]{1,3,2,0:T(8,128)S(1)}, f32[2,6,1,256]{1,3,2,0:T(8,128)S(1)}, u32[]{:S(2)}, u32[]{:S(2)}) collective-permute-start(f32[2,6,1,256]{1,3,2,0:T(8,128)S(1)} %copy.201), channel_id=1, source_target_pairs={{0,1},{2,3},{4,5},{6,7},{8,9},{10,11},{12,13},{14,15},{16,17},{18,... | collective-permute-start | bytes 36872 | tf_op jit(solution)/shard_map/ppermute | solution.py:22
where the time goes:
time: 257 us; the launch traced here: 256 us
  blocking collectives  123 us (48%)
  starting transfers between devices  57.3 us (22%)
  local copies, waits for them, and re-layouts  34.9 us (14%)
  other arithmetic  15.8 us (6%)
  between operations  12.1 us (5%)
  matrix products  8.66 us (3%)
  waiting for transfers between devices  3.97 us (2%)
    psum x2, blocking collectives, on_device(): lax.psum((primal_sq, dual_sq), ('pipe', 'hour', 'seg'))  65.5 us
    all_gather x4, blocking collectives, other_half(): lax.all_gather(edge_row[:, None, :], ('pipe', 'seg'), axis=1, tiled=True)  57.8 us
    ppermute x8, starting transfers between devices, padded(): lax.ppermute(tail, axis, [(i, (i + 1) % count) for i in range(ends)])  27.9 us
    unnamed x55, local copies, waits for them, and re-layouts  17 us
    all_to_all x2, starting transfers between devices, on_device(): lax.all_to_all(hour_spread, 'pipe', split_axis=2, concat_axis=1, tiled=True)  10.8 us
    ppermute x8, starting transfers between devices, padded(): lax.ppermute(head, axis, [((i + 1) % count, i) for i in range(ends)])  10.6 us
    all_to_all x2, starting transfers between devices, on_device(): lax.all_to_all(pack_bar, 'pipe', split_axis=1, concat_axis=2, tiled=True)  7.96 us
  transfers between devices with their start and end apart: 20, of which 3 were waited for; matrix products, arithmetic and copies ran while one was open for 16% of the time, Pallas kernels for 0%

commit v1 on v0

--- a/solution.py
+++ b/solution.py
@@ -33,7 +33,28 @@
 
 
 def other_half(edge_row, half_index, partner_local):
-    gathered = lax.all_gather(edge_row[:, None, :], ("pipe", "seg"), axis=1, tiled=True)
+    x = edge_row[:, None, :]
+    size, index, rows = (
+        lax.axis_size(("pipe", "seg")),
+        lax.axis_index(("pipe", "seg")),
+        x.shape[1],
+    )
+    right = [(i_2, (i_2 + 1) % size) for i_2 in range(size)]
+    left = [(i_2, (i_2 - 1) % size) for i_2 in range(size)]
+    gathered = jnp.zeros((*x.shape[:1], size * rows, *x.shape[1 + 1 :]), x.dtype)
+    gathered = lax.dynamic_update_slice_in_dim(gathered, x, index * rows, axis=1)
+    from_left = from_right = x
+    half = size // 2
+    for step in range(1, half + 1):
+        from_left = lax.ppermute(from_left, ("pipe", "seg"), right)
+        gathered = lax.dynamic_update_slice_in_dim(
+            gathered, from_left, (index - step) % size * rows, axis=1
+        )
+        if step < size - half:
+            from_right = lax.ppermute(from_right, ("pipe", "seg"), left)
+            gathered = lax.dynamic_update_slice_in_dim(
+                gathered, from_right, (index + step) % size * rows, axis=1
+            )
     hour_rows, row_count, row_width = gathered.shape
     seg_count = lax.axis_size("seg")
     picked = gathered.reshape(hour_rows, row_count // seg_count, seg_count, row_width)[

time: 257 us -> 267 us (1.039)
  blocking collectives: 123 us -> 64.1 us
  starting transfers between devices: 57.3 us -> 92.7 us
  waiting for transfers between devices: 3.97 us -> 33.7 us
  local copies, waits for them, and re-layouts: 34.9 us -> 37.7 us
    all_gather x4 -> x0, blocking collectives: 57.8 us -> none  [other_half(): lax.all_gather(edge_row[:, None, :], ('pipe', 'seg'), axis=1, tiled=True)]
    ppermute x0 -> x28, starting transfers between devices: none -> 43.6 us  [the longest x12 42.4 us: other_half(): from_right = lax.ppermute(from_right, ('pipe', 'seg'), left)]
    ppermute x0 -> x28, waiting for transfers between devices: none -> 29.6 us  [the longest x16 29.2 us: other_half(): from_left = lax.ppermute(from_left, ('pipe', 'seg'), right)]
    all_to_all x2, starting transfers between devices: 10.8 us -> 6.9 us  [on_device(): lax.all_to_all(hour_spread, 'pipe', split_axis=2, concat_axis=1, tiled=True)]
    unnamed x55 -> x48, local copies, waits for them, and re-layouts: 17 us -> 17 us
  transfers between devices with their start and end apart: 20 -> 48, of which waited for: 3 -> 15; matrix products, arithmetic and copies ran while one was open for 16% -> 21% of each run, Pallas kernels for 0% -> 0%
where the time goes in v1:
time: 267 us; the launch traced here: 266 us
  starting transfers between devices  92.7 us (35%)
  blocking collectives  64.1 us (24%)
  local copies, waits for them, and re-layouts  37.7 us (14%)
  waiting for transfers between devices  33.7 us (13%)
  other arithmetic  16.4 us (6%)
  between operations  12.2 us (5%)
  matrix products  8.91 us (3%)
    psum x2, blocking collectives, on_device(): lax.psum((primal_sq, dual_sq), ('pipe', 'hour', 'seg'))  64.1 us
    ppermute x12, starting transfers between devices, other_half(): from_right = lax.ppermute(from_right, ('pipe', 'seg'), left)  42.4 us
    ppermute x16, waiting for transfers between devices, other_half(): from_left = lax.ppermute(from_left, ('pipe', 'seg'), right)  29.2 us
    ppermute x8, starting transfers between devices, padded(): lax.ppermute(tail, axis, [(i, (i + 1) % count) for i in range(ends)])  25.3 us
    unnamed x48, local copies, waits for them, and re-layouts  17 us
    ppermute x8, starting transfers between devices, padded(): lax.ppermute(head, axis, [((i + 1) % count, i) for i in range(ends)])  10.3 us
    all_to_all x2, starting transfers between devices, on_device(): lax.all_to_all(hour_spread, 'pipe', split_axis=2, concat_axis=1, tiled=True)  6.9 us
    all_to_all x2, starting transfers between devices, on_device(): lax.all_to_all(pack_bar, 'pipe', split_axis=1, concat_axis=2, tiled=True)  6.66 us
  transfers between devices with their start and end apart: 48, of which 15 were waited for; matrix products, arithmetic and copies ran while one was open for 21% of the time, Pallas kernels for 0%

profile of v1, /device:TPU:0, one launch (start us, length us, event | category | flops | bytes accessed | tf_op | source)
XLA Modules:
  0.0 265.7 jit_solution(11032236407211072517)
XLA Ops:
  1.8 4.0 %collective-permute-start.4 = (f32[4,1,256]{2,1,0:T(1,128)S(1)}, f32[4,1,256]{2,1,0:T(1,128)S(1)}, u32[]{:S(2)}, u32[]{:S(2)}) collective-permute-start(f32[4,1,256]{2,1,0:T(1,128)S(1)} %slice.129), channel_id=1, source_target_pairs={{0,13},{1,0},{4,1},{5,4},{8,5},{9,8},{12,9},{13,12},{2,15},{3,2},{... | collective-permute-start | bytes 12296 | tf_op jit(solution)/shard_map/ppermute | solution.py:54
  5.9 2.2 fusion.4
  9.0 3.1 %reshape.116 = f32[4,1,8192]{2,1,0:T(1,128)} reshape(f32[1024,4,8]{2,1,0:T(4,128)S(1)} %bitcast.195) | data formatting | bytes 262144
  12.1 3.6 %all-to-all-start = ((f32[4,1,8192]{2,1,0:T(1,128)}), f32[4,1,8192]{2,1,0:T(1,128)S(1)}, u32[]{:S(2)}, u32[]{:S(2)}) async-start(f32[4,1,8192]{2,1,0:T(1,128)} %reshape.116), calls=%async_computation | async-start | bytes 262144 | tf_op jit(solution)/shard_map/all_to_all | solution.py:162
  15.6 1.3 collective-permute-start.1
  16.9 4.5 %collective-permute-start = (f32[2,1,32,256]{3,2,1,0:T(8,128)S(1)}, f32[2,1,32,256]{3,2,1,0:T(8,128)S(1)}, u32[]{:S(2)}, u32[]{:S(2)}) collective-permute-start(f32[2,1,32,256]{3,2,1,0:T(8,128)S(1)} %get-tuple-element.141), channel_id=1, source_target_pairs={{0,2},{1,3},{4,6},{5,7},{8,10},{9,11},{12,14},{13,15},{16,18},{17,... | collective-permute-start | bytes 196616 | tf_op jit(solution)/shard_map/ppermute | solution.py:22
  21.7 4.3 %scatter_custom_fusion = s32[1024]{0:T(1024)S(1)} fusion(s32[1024]{0:T(1024)S(1)} %compare_select_fusion, s32[1024]{0:T(1024)S(1)} %iota.14, s32[]{:T(128)} %constant.152.clone.1), kind=kCustom, calls=%fused_computation.172 | custom fusion | bytes 4100 | tf_op jit(solution)/shard_map/scatter | solution.py:143
  27.1 3.5 %collective-permute-start.6 = (f32[4,1,256]{2,1,0:T(1,128)S(1)}, f32[4,1,256]{2,1,0:T(1,128)S(1)}, u32[]{:S(2)}, u32[]{:S(2)}) collective-permute-start(f32[4,1,256]{2,1,0:T(1,128)S(1)} %collective-permute-done.4), channel_id=1, source_target_pairs={{0,13},{1,0},{4,1},{5,4},{8,5},{9,8},{12,9},{13,12},{2,15},{3,2},{... | collective-permute-start | bytes 12296 | tf_op jit(solution)/shard_map/ppermute | solution.py:54
  30.7 1.3 collective-permute-done.5
  32.0 3.5 %collective-permute-start.8 = (f32[4,1,256]{2,1,0:T(1,128)S(1)}, f32[4,1,256]{2,1,0:T(1,128)S(1)}, u32[]{:S(2)}, u32[]{:S(2)}) collective-permute-start(f32[4,1,256]{2,1,0:T(1,128)S(1)} %collective-permute-done.6), channel_id=1, source_target_pairs={{0,13},{1,0},{4,1},{5,4},{8,5},{9,8},{12,9},{13,12},{2,15},{3,2},{... | collective-permute-start | bytes 12296 | tf_op jit(solution)/shard_map/ppermute | solution.py:54
  35.5 1.3 collective-permute-done.7
  36.8 4.8 %collective-permute-done.9 = f32[4,1,256]{2,1,0:T(1,128)S(1)} collective-permute-done((f32[4,1,256]{2,1,0:T(1,128)S(1)}, f32[4,1,256]{2,1,0:T(1,128)S(1)}, u32[]{:S(2)}, u32[]{:S(2)}) %collective-permute-start.9) | collective-permute-done | bytes 4128 | tf_op jit(solution)/shard_map/ppermute | solution.py:49
  42.9 1.3 collective-permute-start.10
  44.4 1.3 collective-permute-start.2
  46.3 1.5 collective-permute-done.2
  49.5 2.5 reshape.117
  52.0 1.8 broadcast_multiply_fusion.1
  53.9 1.9 copy.242
  57.4 3.4 %collective-permute-start.15 = (f32[4,1,256]{2,0,1:T(4,128)S(1)}, f32[4,1,256]{2,0,1:T(4,128)S(1)}, u32[]{:S(2)}, u32[]{:S(2)}) collective-permute-start(f32[4,1,256]{2,0,1:T(4,128)S(1)} %get-tuple-element.147), channel_id=1, source_target_pairs={{0,13},{1,0},{4,1},{5,4},{8,5},{9,8},{12,9},{13,12},{2,15},{3,2},{... | collective-permute-start | bytes 12296 | tf_op jit(solution)/shard_map/ppermute | solution.py:54
  61.6 3.3 %all-to-all-start.1 = ((f32[4,32,256]{2,0,1:T(4,128)}), f32[4,32,256]{2,0,1:T(4,128)S(1)}, u32[]{:S(2)}, u32[]{:S(2)}) async-start(f32[4,32,256]{2,0,1:T(4,128)} %multiply_subtract_fusion.3), calls=%async_computation.1 | async-start | bytes 262144 | tf_op jit(solution)/shard_map/all_to_all | solution.py:180
  65.9 1.3 collective-permute-start.12
  67.2 4.5 %collective-permute-start.11 = (f32[2,1,32,256]{3,2,1,0:T(8,128)S(1)}, f32[2,1,32,256]{3,2,1,0:T(8,128)S(1)}, u32[]{:S(2)}, u32[]{:S(2)}) collective-permute-start(f32[2,1,32,256]{3,2,1,0:T(8,128)S(1)} %get-tuple-element.137), channel_id=1, source_target_pairs={{0,2},{1,3},{4,6},{5,7},{8,10},{9,11},{12,14},{13,15},{16,18},{17,... | collective-permute-start | bytes 196616 | tf_op jit(solution)/shard_map/ppermute | solution.py:22
  73.2 3.5 %collective-permute-start.17 = (f32[4,1,256]{2,0,1:T(4,128)S(1)}, f32[4,1,256]{2,0,1:T(4,128)S(1)}, u32[]{:S(2)}, u32[]{:S(2)}) collective-permute-start(f32[4,1,256]{2,0,1:T(4,128)S(1)} %collective-permute-done.15), channel_id=1, source_target_pairs={{0,13},{1,0},{4,1},{5,4},{8,5},{9,8},{12,9},{13,12},{2,15},{3,2},{... | collective-permute-start | bytes 12296 | tf_op jit(solution)/shard_map/ppermute | solution.py:54
  76.7 1.3 collective-permute-done.16
  78.0 3.5 %collective-permute-start.19 = (f32[4,1,256]{2,0,1:T(4,128)S(1)}, f32[4,1,256]{2,0,1:T(4,128)S(1)}, u32[]{:S(2)}, u32[]{:S(2)}) collective-permute-start(f32[4,1,256]{2,0,1:T(4,128)S(1)} %collective-permute-done.17), channel_id=1, source_target_pairs={{0,13},{1,0},{4,1},{5,4},{8,5},{9,8},{12,9},{13,12},{2,15},{3,2},{... | collective-permute-start | bytes 12296 | tf_op jit(solution)/shard_map/ppermute | solution.py:54
  81.6 1.3 collective-permute-done.18
  82.9 4.8 %collective-permute-done.20 = f32[4,1,256]{2,0,1:T(4,128)S(1)} collective-permute-done((f32[4,1,256]{2,0,1:T(4,128)S(1)}, f32[4,1,256]{2,0,1:T(4,128)S(1)}, u32[]{:S(2)}, u32[]{:S(2)}) %collective-permute-start.20) | collective-permute-done | bytes 4128 | tf_op jit(solution)/shard_map/ppermute | solution.py:49
  89.1 1.5 collective-permute-start.13
  90.6 1.3 collective-permute-start.21
  92.2 1.5 collective-permute-done.21
  93.7 1.9 multiply_reduce_fusion.7
  95.9 3.4 %collective-permute-start.26 = (f32[4,1,256]{2,0,1:T(4,128)S(1)}, f32[4,1,256]{2,0,1:T(4,128)S(1)}, u32[]{:S(2)}, u32[]{:S(2)}) collective-permute-start(f32[4,1,256]{2,0,1:T(4,128)S(1)} %get-tuple-element.145), channel_id=1, source_target_pairs={{0,13},{1,0},{4,1},{5,4},{8,5},{9,8},{12,9},{13,12},{2,15},{3,2},{... | collective-permute-start | bytes 12296 | tf_op jit(solution)/shard_map/ppermute | solution.py:54
  100.0 1.3 collective-permute-start.23
  101.3 4.5 %collective-permute-start.22 = (f32[2,1,32,256]{3,2,1,0:T(8,128)S(1)}, f32[2,1,32,256]{3,2,1,0:T(8,128)S(1)}, u32[]{:S(2)}, u32[]{:S(2)}) collective-permute-start(f32[2,1,32,256]{3,2,1,0:T(8,128)S(1)} %get-tuple-element.133), channel_id=1, source_target_pairs={{0,2},{1,3},{4,6},{5,7},{8,10},{9,11},{12,14},{13,15},{16,18},{17,... | collective-permute-start | bytes 196616 | tf_op jit(solution)/shard_map/ppermute | solution.py:22
  107.3 3.5 %collective-permute-start.28 = (f32[4,1,256]{2,0,1:T(4,128)S(1)}, f32[4,1,256]{2,0,1:T(4,128)S(1)}, u32[]{:S(2)}, u32[]{:S(2)}) collective-permute-start(f32[4,1,256]{2,0,1:T(4,128)S(1)} %collective-permute-done.26), channel_id=1, source_target_pairs={{0,13},{1,0},{4,1},{5,4},{8,5},{9,8},{12,9},{13,12},{2,15},{3,2},{... | collective-permute-start | bytes 12296 | tf_op jit(solution)/shard_map/ppermute | solution.py:54
  112.1 3.5 %collective-permute-start.30 = (f32[4,1,256]{2,0,1:T(4,128)S(1)}, f32[4,1,256]{2,0,1:T(4,128)S(1)}, u32[]{:S(2)}, u32[]{:S(2)}) collective-permute-start(f32[4,1,256]{2,0,1:T(4,128)S(1)} %collective-permute-done.28), channel_id=1, source_target_pairs={{0,13},{1,0},{4,1},{5,4},{8,5},{9,8},{12,9},{13,12},{2,15},{3,2},{... | collective-permute-start | bytes 12296 | tf_op jit(solution)/shard_map/ppermute | solution.py:54
  115.6 1.3 collective-permute-done.29
  116.9 4.8 %collective-permute-done.31 = f32[4,1,256]{2,0,1:T(4,128)S(1)} collective-permute-done((f32[4,1,256]{2,0,1:T(4,128)S(1)}, f32[4,1,256]{2,0,1:T(4,128)S(1)}, u32[]{:S(2)}, u32[]{:S(2)}) %collective-permute-start.31) | collective-permute-done | bytes 4128 | tf_op jit(solution)/shard_map/ppermute | solution.py:49
  122.0 1.3 gather_fusion.2
  123.6 1.3 collective-permute-start.32
  125.8 1.3 collective-permute-start.24
  127.2 2.2 fusion.73
  129.4 2.1 fusion.1
  131.5 1.6 copy.271
  133.1 3.1 %reshape.118 = f32[4,1,8192]{2,1,0:T(1,128)} reshape(f32[1024,4,8]{2,1,0:T(4,128)S(1)} %bitcast.197) | data formatting | bytes 262144
  136.2 3.3 %all-to-all-start.2 = ((f32[4,1,8192]{2,1,0:T(1,128)}), f32[4,1,8192]{2,1,0:T(1,128)S(1)}, u32[]{:S(2)}, u32[]{:S(2)}) async-start(f32[4,1,8192]{2,1,0:T(1,128)} %reshape.118), calls=%async_computation.2 | async-start | bytes 262144 | tf_op jit(solution)/shard_map/all_to_all | solution.py:162
  141.4 33.7 %all-reduce.1 = (f32[]{:T(128)}, f32[]{:T(128)}) all-reduce(f32[]{:T(128)S(6)} %add.291, f32[]{:T(128)S(6)} %add.293), channel_id=1, replica_groups=mesh['groups'=2,'pipe'=4,'hour'=2,'seg'=2] {'pipe','hour','seg'}, use_global_device_ids=true, to_apply=%region_5.7 | all-reduce | flops 2 | bytes 16 | tf_op jit(solution)/shard_map/psum | solution.py:192
  176.6 1.6 reduce.1
  178.2 3.4 %reshape.119 = f32[1024,4,8]{2,1,0:T(4,128)S(1)} reshape(f32[4,8192]{1,0:T(4,128)} %reduce.1) | data formatting | bytes 262144
  181.6 1.8 broadcast_multiply_fusion
  183.5 1.9 copy.272
  188.5 3.5 %collective-permute-start.37 = (f32[4,1,256]{2,0,1:T(4,128)S(1)}, f32[4,1,256]{2,0,1:T(4,128)S(1)}, u32[]{:S(2)}, u32[]{:S(2)}) collective-permute-start(f32[4,1,256]{2,0,1:T(4,128)S(1)} %get-tuple-element.143), channel_id=1, source_target_pairs={{0,13},{1,0},{4,1},{5,4},{8,5},{9,8},{12,9},{13,12},{2,15},{3,2},{... | collective-permute-start | bytes 12296 | tf_op jit(solution)/shard_map/ppermute | solution.py:54
  192.1 3.3 %all-to-all-start.3 = ((f32[4,32,256]{2,0,1:T(4,128)}), f32[4,32,256]{2,0,1:T(4,128)S(1)}, u32[]{:S(2)}, u32[]{:S(2)}) async-start(f32[4,32,256]{2,0,1:T(4,128)} %multiply_subtract_fusion.1), calls=%async_computation.3 | async-start | bytes 262144 | tf_op jit(solution)/shard_map/all_to_all | solution.py:180
  196.4 1.3 collective-permute-start.34
  197.7 4.5 %collective-permute-start.33 = (f32[2,1,32,256]{3,2,1,0:T(8,128)S(1)}, f32[2,1,32,256]{3,2,1,0:T(8,128)S(1)}, u32[]{:S(2)}, u32[]{:S(2)}) collective-permute-start(f32[2,1,32,256]{3,2,1,0:T(8,128)S(1)} %get-tuple-element.129), channel_id=1, source_target_pairs={{0,2},{1,3},{4,6},{5,7},{8,10},{9,11},{12,14},{13,15},{16,18},{17,... | collective-permute-start | bytes 196616 | tf_op jit(solution)/shard_map/ppermute | solution.py:22
  203.7 3.5 %collective-permute-start.39 = (f32[4,1,256]{2,0,1:T(4,128)S(1)}, f32[4,1,256]{2,0,1:T(4,128)S(1)}, u32[]{:S(2)}, u32[]{:S(2)}) collective-permute-start(f32[4,1,256]{2,0,1:T(4,128)S(1)} %collective-permute-done.37), channel_id=1, source_target_pairs={{0,13},{1,0},{4,1},{5,4},{8,5},{9,8},{12,9},{13,12},{2,15},{3,2},{... | collective-permute-start | bytes 12296 | tf_op jit(solution)/shard_map/ppermute | solution.py:54
  208.5 3.5 %collective-permute-start.41 = (f32[4,1,256]{2,0,1:T(4,128)S(1)}, f32[4,1,256]{2,0,1:T(4,128)S(1)}, u32[]{:S(2)}, u32[]{:S(2)}) collective-permute-start(f32[4,1,256]{2,0,1:T(4,128)S(1)} %collective-permute-done.39), channel_id=1, source_target_pairs={{0,13},{1,0},{4,1},{5,4},{8,5},{9,8},{12,9},{13,12},{2,15},{3,2},{... | collective-permute-start | bytes 12296 | tf_op jit(solution)/shard_map/ppermute | solution.py:54
  212.1 1.3 collective-permute-done.40
  213.4 4.8 %collective-permute-done.42 = f32[4,1,256]{2,0,1:T(4,128)S(1)} collective-permute-done((f32[4,1,256]{2,0,1:T(4,128)S(1)}, f32[4,1,256]{2,0,1:T(4,128)S(1)}, u32[]{:S(2)}, u32[]{:S(2)}) %collective-permute-start.42) | collective-permute-done | bytes 4128 | tf_op jit(solution)/shard_map/ppermute | solution.py:49
  219.5 1.3 collective-permute-start.43
  220.9 3.0 %collective-permute-start.35 = (f32[2,6,1,256]{1,3,2,0:T(8,128)S(1)}, f32[2,6,1,256]{1,3,2,0:T(8,128)S(1)}, u32[]{:S(2)}, u32[]{:S(2)}) collective-permute-start(f32[2,6,1,256]{1,3,2,0:T(8,128)S(1)} %copy.295), channel_id=1, source_target_pairs={{0,1},{2,3},{4,5},{6,7},{8,9},{10,11},{12,13},{14,15},{16,17},{18,... | collective-permute-start | bytes 36872 | tf_op jit(solution)/shard_map/ppermute | solution.py:22
  225.3 1.8 multiply_reduce_fusion.2
  229.2 2.4 multiply_reduce_fusion.8
  232.9 30.3 %all-reduce = (f32[]{:T(128)}, f32[]{:T(128)}) all-reduce(f32[]{:T(128)S(6)} %add.305, f32[]{:T(128)S(6)} %add.307), channel_id=1, replica_groups=mesh['groups'=2,'pipe'=4,'hour'=2,'seg'=2] {'pipe','hour','seg'}, use_global_device_ids=true, to_apply=%region_12.14 | all-reduce | flops 2 | bytes 16 | tf_op jit(solution)/shard_map/psum | solution.py:192
  (201 shorter events, 27.0 us)
Async XLA Ops:
  1.4 25.7 %collective-permute-start.3 = (f32[4,1,256]{2,1,0:T(1,128)S(1)}, f32[4,1,256]{2,1,0:T(1,128)S(1)}, u32[]{:S(2)}, u32[]{:S(2)}) collective-permute-start(f32[4,1,256]{2,1,0:T(1,128)S(1)} %slice.129), channel_id=1, source_target_pairs={{0,1},{1,4},{4,5},{5,8},{8,9},{9,12},{12,13},{13,0},{2,3},{3,6},{6... | collective-permute-start | bytes 12296 | tf_op jit(solution)/shard_map/ppermute | solution.py:49
  1.8 25.3 %collective-permute-start.4 = (f32[4,1,256]{2,1,0:T(1,128)S(1)}, f32[4,1,256]{2,1,0:T(1,128)S(1)}, u32[]{:S(2)}, u32[]{:S(2)}) collective-permute-start(f32[4,1,256]{2,1,0:T(1,128)S(1)} %slice.129), channel_id=1, source_target_pairs={{0,13},{1,0},{4,1},{5,4},{8,5},{9,8},{12,9},{13,12},{2,15},{3,2},{... | collective-permute-start | bytes 12296 | tf_op jit(solution)/shard_map/ppermute | solution.py:54
  8.1 7.6 %copy-start = (f32[4,32,256]{2,1,0:T(8,128)S(1)}, f32[4,32,256]{2,1,0:T(8,128)}, u32[]{:S(2)}) copy-start(f32[4,32,256]{2,1,0:T(8,128)} %param.16) | copy-start | bytes 393220
  8.1 7.6 %copy-start.1 = (f32[4,32,256]{2,1,0:T(8,128)S(1)}, f32[4,32,256]{2,1,0:T(8,128)}, u32[]{:S(2)}) copy-start(f32[4,32,256]{2,1,0:T(8,128)} %param.17) | copy-start | bytes 393220
  8.1 13.5 %copy-start.11 = (s32[1024]{0:T(1024)S(1)}, s32[1024]{0:T(1024)}, u32[]{:S(2)}) copy-start(s32[1024]{0:T(1024)} %param.24) | copy-start | bytes 12292
  8.1 18.0 %copy-start.10 = (s32[32,256]{1,0:T(8,128)S(1)}, s32[32,256]{1,0:T(8,128)}, u32[]{:S(2)}) copy-start(s32[32,256]{1,0:T(8,128)} %param.23) | copy-start | bytes 98308
  8.1 18.0 %copy-start.12 = (f32[16]{0:T(128)S(1)}, f32[16]{0:T(128)}, u32[]{:S(2)}) copy-start(f32[16]{0:T(128)} %param.22) | copy-start | bytes 196
  12.1 35.9 %all-to-all-start = ((f32[4,1,8192]{2,1,0:T(1,128)}), f32[4,1,8192]{2,1,0:T(1,128)S(1)}, u32[]{:S(2)}, u32[]{:S(2)}) async-start(f32[4,1,8192]{2,1,0:T(1,128)} %reshape.116), calls=%async_computation | async-start | bytes 262144 | tf_op jit(solution)/shard_map/all_to_all | solution.py:162
  15.6 26.9 %collective-permute-start.1 = (f32[2,1,32,256]{3,2,1,0:T(8,128)S(1)}, f32[2,1,32,256]{3,2,1,0:T(8,128)S(1)}, u32[]{:S(2)}, u32[]{:S(2)}) collective-permute-start(f32[2,1,32,256]{3,2,1,0:T(8,128)S(1)} %get-tuple-element.142), channel_id=1, source_target_pairs={{2,0},{3,1},{6,4},{7,5},{10,8},{11,9},{14,12},{15,13},{18,16},{19,... | collective-permute-start | bytes 196616 | tf_op jit(solution)/shard_map/ppermute | solution.py:24
  16.9 25.6 %collective-permute-start = (f32[2,1,32,256]{3,2,1,0:T(8,128)S(1)}, f32[2,1,32,256]{3,2,1,0:T(8,128)S(1)}, u32[]{:S(2)}, u32[]{:S(2)}) collective-permute-start(f32[2,1,32,256]{3,2,1,0:T(8,128)S(1)} %get-tuple-element.141), channel_id=1, source_target_pairs={{0,2},{1,3},{4,6},{5,7},{8,10},{9,11},{12,14},{13,15},{16,18},{17,... | collective-permute-start | bytes 196616 | tf_op jit(solution)/shard_map/ppermute | solution.py:22
  27.1 4.8 %collective-permute-start.5 = (f32[4,1,256]{2,1,0:T(1,128)S(1)}, f32[4,1,256]{2,1,0:T(1,128)S(1)}, u32[]{:S(2)}, u32[]{:S(2)}) collective-permute-start(f32[4,1,256]{2,1,0:T(1,128)S(1)} %collective-permute-done.3), channel_id=1, source_target_pairs={{0,1},{1,4},{4,5},{5,8},{8,9},{9,12},{12,13},{13,0},{2,3},{3,6},{6... | collective-permute-start | bytes 12296 | tf_op jit(solution)/shard_map/ppermute | solution.py:49
  27.1 4.9 %collective-permute-start.6 = (f32[4,1,256]{2,1,0:T(1,128)S(1)}, f32[4,1,256]{2,1,0:T(1,128)S(1)}, u32[]{:S(2)}, u32[]{:S(2)}) collective-permute-start(f32[4,1,256]{2,1,0:T(1,128)S(1)} %collective-permute-done.4), channel_id=1, source_target_pairs={{0,13},{1,0},{4,1},{5,4},{8,5},{9,8},{12,9},{13,12},{2,15},{3,2},{... | collective-permute-start | bytes 12296 | tf_op jit(solution)/shard_map/ppermute | solution.py:54
  31.9 4.8 %collective-permute-start.7 = (f32[4,1,256]{2,1,0:T(1,128)S(1)}, f32[4,1,256]{2,1,0:T(1,128)S(1)}, u32[]{:S(2)}, u32[]{:S(2)}) collective-permute-start(f32[4,1,256]{2,1,0:T(1,128)S(1)} %collective-permute-done.5), channel_id=1, source_target_pairs={{0,1},{1,4},{4,5},{5,8},{8,9},{9,12},{12,13},{13,0},{2,3},{3,6},{6... | collective-permute-start | bytes 12296 | tf_op jit(solution)/shard_map/ppermute | solution.py:49
  32.0 4.8 %collective-permute-start.8 = (f32[4,1,256]{2,1,0:T(1,128)S(1)}, f32[4,1,256]{2,1,0:T(1,128)S(1)}, u32[]{:S(2)}, u32[]{:S(2)}) collective-permute-start(f32[4,1,256]{2,1,0:T(1,128)S(1)} %collective-permute-done.6), channel_id=1, source_target_pairs={{0,13},{1,0},{4,1},{5,4},{8,5},{9,8},{12,9},{13,12},{2,15},{3,2},{... | collective-permute-start | bytes 12296 | tf_op jit(solution)/shard_map/ppermute | solution.py:54
  36.8 4.8 %collective-permute-start.9 = (f32[4,1,256]{2,1,0:T(1,128)S(1)}, f32[4,1,256]{2,1,0:T(1,128)S(1)}, u32[]{:S(2)}, u32[]{:S(2)}) collective-permute-start(f32[4,1,256]{2,1,0:T(1,128)S(1)} %collective-permute-done.7), channel_id=1, source_target_pairs={{0,1},{1,4},{4,5},{5,8},{8,9},{9,12},{12,13},{13,0},{2,3},{3,6},{6... | collective-permute-start | bytes 12296 | tf_op jit(solution)/shard_map/ppermute | solution.py:49
  42.9 12.9 %collective-permute-start.10 = (f32[2,6,1,256]{3,1,2,0:T(8,128)S(1)}, f32[2,6,1,256]{3,1,2,0:T(8,128)S(1)}, u32[]{:S(2)}, u32[]{:S(2)}) collective-permute-start(f32[2,6,1,256]{3,1,2,0:T(8,128)S(1)} %slice.176), channel_id=1, source_target_pairs={{0,1},{2,3},{4,5},{6,7},{8,9},{10,11},{12,13},{14,15},{16,17},{18,... | collective-permute-start | bytes 36872 | tf_op jit(solution)/shard_map/ppermute | solution.py:22
  44.4 3.4 %collective-permute-start.2 = (f32[2,6,1,256]{1,3,2,0:T(8,128)S(1)}, f32[2,6,1,256]{1,3,2,0:T(8,128)S(1)}, u32[]{:S(2)}, u32[]{:S(2)}) collective-permute-start(f32[2,6,1,256]{1,3,2,0:T(8,128)S(1)} %copy.288), channel_id=1, source_target_pairs={{1,0},{3,2},{5,4},{7,6},{9,8},{11,10},{13,12},{15,14},{17,16},{19,... | collective-permute-start | bytes 36872 | tf_op jit(solution)/shard_map/ppermute | solution.py:24
  53.9 1.9 copy-start.2
  53.9 2.0 copy-start.3
  53.9 2.0 copy-start.4
  53.9 2.0 copy-start.7
  53.9 2.0 copy-start.8
  57.2 15.9 %collective-permute-start.14 = (f32[4,1,256]{2,0,1:T(4,128)S(1)}, f32[4,1,256]{2,0,1:T(4,128)S(1)}, u32[]{:S(2)}, u32[]{:S(2)}) collective-permute-start(f32[4,1,256]{2,0,1:T(4,128)S(1)} %get-tuple-element.147), channel_id=1, source_target_pairs={{0,1},{1,4},{4,5},{5,8},{8,9},{9,12},{12,13},{13,0},{2,3},{3,6},{6... | collective-permute-start | bytes 12296 | tf_op jit(solution)/shard_map/ppermute | solution.py:49
  57.4 15.8 %collective-permute-start.15 = (f32[4,1,256]{2,0,1:T(4,128)S(1)}, f32[4,1,256]{2,0,1:T(4,128)S(1)}, u32[]{:S(2)}, u32[]{:S(2)}) collective-permute-start(f32[4,1,256]{2,0,1:T(4,128)S(1)} %get-tuple-element.147), channel_id=1, source_target_pairs={{0,13},{1,0},{4,1},{5,4},{8,5},{9,8},{12,9},{13,12},{2,15},{3,2},{... | collective-permute-start | bytes 12296 | tf_op jit(solution)/shard_map/ppermute | solution.py:54
  61.6 65.5 %all-to-all-start.1 = ((f32[4,32,256]{2,0,1:T(4,128)}), f32[4,32,256]{2,0,1:T(4,128)S(1)}, u32[]{:S(2)}, u32[]{:S(2)}) async-start(f32[4,32,256]{2,0,1:T(4,128)} %multiply_subtract_fusion.3), calls=%async_computation.1 | async-start | bytes 262144 | tf_op jit(solution)/shard_map/all_to_all | solution.py:180
  64.9 28.7 %copy-start.5 = (f32[4,32,256]{2,1,0:T(8,128)S(1)}, f32[4,32,256]{2,1,0:T(8,128)}, u32[]{:S(2)}) copy-start(f32[4,32,256]{2,1,0:T(8,128)} %param.20) | copy-start | bytes 393220
  65.9 22.7 %collective-permute-start.12 = (f32[2,1,32,256]{3,2,1,0:T(8,128)S(1)}, f32[2,1,32,256]{3,2,1,0:T(8,128)S(1)}, u32[]{:S(2)}, u32[]{:S(2)}) collective-permute-start(f32[2,1,32,256]{3,2,1,0:T(8,128)S(1)} %get-tuple-element.138), channel_id=1, source_target_pairs={{2,0},{3,1},{6,4},{7,5},{10,8},{11,9},{14,12},{15,13},{18,16},{19,... | collective-permute-start | bytes 196616 | tf_op jit(solution)/shard_map/ppermute | solution.py:24
  67.2 21.4 %collective-permute-start.11 = (f32[2,1,32,256]{3,2,1,0:T(8,128)S(1)}, f32[2,1,32,256]{3,2,1,0:T(8,128)S(1)}, u32[]{:S(2)}, u32[]{:S(2)}) collective-permute-start(f32[2,1,32,256]{3,2,1,0:T(8,128)S(1)} %get-tuple-element.137), channel_id=1, source_target_pairs={{0,2},{1,3},{4,6},{5,7},{8,10},{9,11},{12,14},{13,15},{16,18},{17,... | collective-permute-start | bytes 196616 | tf_op jit(solution)/shard_map/ppermute | solution.py:22
  73.1 4.9 %collective-permute-start.16 = (f32[4,1,256]{2,0,1:T(4,128)S(1)}, f32[4,1,256]{2,0,1:T(4,128)S(1)}, u32[]{:S(2)}, u32[]{:S(2)}) collective-permute-start(f32[4,1,256]{2,0,1:T(4,128)S(1)} %collective-permute-done.14), channel_id=1, source_target_pairs={{0,1},{1,4},{4,5},{5,8},{8,9},{9,12},{12,13},{13,0},{2,3},{3,6},{6... | collective-permute-start | bytes 12296 | tf_op jit(solution)/shard_map/ppermute | solution.py:49
  73.2 4.8 %collective-permute-start.17 = (f32[4,1,256]{2,0,1:T(4,128)S(1)}, f32[4,1,256]{2,0,1:T(4,128)S(1)}, u32[]{:S(2)}, u32[]{:S(2)}) collective-permute-start(f32[4,1,256]{2,0,1:T(4,128)S(1)} %collective-permute-done.15), channel_id=1, source_target_pairs={{0,13},{1,0},{4,1},{5,4},{8,5},{9,8},{12,9},{13,12},{2,15},{3,2},{... | collective-permute-start | bytes 12296 | tf_op jit(solution)/shard_map/ppermute | solution.py:54
  78.0 4.8 %collective-permute-start.18 = (f32[4,1,256]{2,0,1:T(4,128)S(1)}, f32[4,1,256]{2,0,1:T(4,128)S(1)}, u32[]{:S(2)}, u32[]{:S(2)}) collective-permute-start(f32[4,1,256]{2,0,1:T(4,128)S(1)} %collective-permute-done.16), channel_id=1, source_target_pairs={{0,1},{1,4},{4,5},{5,8},{8,9},{9,12},{12,13},{13,0},{2,3},{3,6},{6... | collective-permute-start | bytes 12296 | tf_op jit(solution)/shard_map/ppermute | solution.py:49
  78.0 4.8 %collective-permute-start.19 = (f32[4,1,256]{2,0,1:T(4,128)S(1)}, f32[4,1,256]{2,0,1:T(4,128)S(1)}, u32[]{:S(2)}, u32[]{:S(2)}) collective-permute-start(f32[4,1,256]{2,0,1:T(4,128)S(1)} %collective-permute-done.17), channel_id=1, source_target_pairs={{0,13},{1,0},{4,1},{5,4},{8,5},{9,8},{12,9},{13,12},{2,15},{3,2},{... | collective-permute-start | bytes 12296 | tf_op jit(solution)/shard_map/ppermute | solution.py:54
  82.8 4.8 %collective-permute-start.20 = (f32[4,1,256]{2,0,1:T(4,128)S(1)}, f32[4,1,256]{2,0,1:T(4,128)S(1)}, u32[]{:S(2)}, u32[]{:S(2)}) collective-permute-start(f32[4,1,256]{2,0,1:T(4,128)S(1)} %collective-permute-done.18), channel_id=1, source_target_pairs={{0,1},{1,4},{4,5},{5,8},{8,9},{9,12},{12,13},{13,0},{2,3},{3,6},{6... | collective-permute-start | bytes 12296 | tf_op jit(solution)/shard_map/ppermute | solution.py:49
  89.1 2.8 %collective-permute-start.13 = (f32[2,6,1,256]{1,3,2,0:T(8,128)S(1)}, f32[2,6,1,256]{1,3,2,0:T(8,128)S(1)}, u32[]{:S(2)}, u32[]{:S(2)}) collective-permute-start(f32[2,6,1,256]{1,3,2,0:T(8,128)S(1)} %copy.291), channel_id=1, source_target_pairs={{0,1},{2,3},{4,5},{6,7},{8,9},{10,11},{12,13},{14,15},{16,17},{18,... | collective-permute-start | bytes 36872 | tf_op jit(solution)/shard_map/ppermute | solution.py:22
  90.6 3.1 %collective-permute-start.21 = (f32[2,6,1,256]{3,1,2,0:T(8,128)S(1)}, f32[2,6,1,256]{3,1,2,0:T(8,128)S(1)}, u32[]{:S(2)}, u32[]{:S(2)}) collective-permute-start(f32[2,6,1,256]{3,1,2,0:T(8,128)S(1)} %slice.184), channel_id=1, source_target_pairs={{1,0},{3,2},{5,4},{7,6},{9,8},{11,10},{13,12},{15,14},{17,16},{19,... | collective-permute-start | bytes 36872 | tf_op jit(solution)/shard_map/ppermute | solution.py:24
  95.6 11.5 %collective-permute-start.25 = (f32[4,1,256]{2,0,1:T(4,128)S(1)}, f32[4,1,256]{2,0,1:T(4,128)S(1)}, u32[]{:S(2)}, u32[]{:S(2)}) collective-permute-start(f32[4,1,256]{2,0,1:T(4,128)S(1)} %get-tuple-element.145), channel_id=1, source_target_pairs={{0,1},{1,4},{4,5},{5,8},{8,9},{9,12},{12,13},{13,0},{2,3},{3,6},{6... | collective-permute-start | bytes 12296 | tf_op jit(solution)/shard_map/ppermute | solution.py:49
  95.9 11.4 %collective-permute-start.26 = (f32[4,1,256]{2,0,1:T(4,128)S(1)}, f32[4,1,256]{2,0,1:T(4,128)S(1)}, u32[]{:S(2)}, u32[]{:S(2)}) collective-permute-start(f32[4,1,256]{2,0,1:T(4,128)S(1)} %get-tuple-element.145), channel_id=1, source_target_pairs={{0,13},{1,0},{4,1},{5,4},{8,5},{9,8},{12,9},{13,12},{2,15},{3,2},{... | collective-permute-start | bytes 12296 | tf_op jit(solution)/shard_map/ppermute | solution.py:54
  99.3 27.9 %copy-start.13 = (f32[4,1,8,128]{3,2,1,0:T(8,128)S(1)}, f32[4,1,8,128]{3,2,1,0:T(8,128)}, u32[]{:S(2)}) copy-start(f32[4,1,8,128]{3,2,1,0:T(8,128)} %param.18) | copy-start | bytes 49156
  99.3 27.9 %copy-start.14 = (s32[4,1024]{1,0:T(4,128)S(1)}, s32[4,1024]{1,0:T(4,128)}, u32[]{:S(2)}) copy-start(s32[4,1024]{1,0:T(4,128)} %param.25) | copy-start | bytes 49156
  99.3 27.9 %copy-start.15 = (f32[4,1,8,128]{3,2,1,0:T(8,128)S(1)}, f32[4,1,8,128]{3,2,1,0:T(8,128)}, u32[]{:S(2)}) copy-start(f32[4,1,8,128]{3,2,1,0:T(8,128)} %param.21) | copy-start | bytes 49156
  100.0 23.3 %collective-permute-start.23 = (f32[2,1,32,256]{3,2,1,0:T(8,128)S(1)}, f32[2,1,32,256]{3,2,1,0:T(8,128)S(1)}, u32[]{:S(2)}, u32[]{:S(2)}) collective-permute-start(f32[2,1,32,256]{3,2,1,0:T(8,128)S(1)} %get-tuple-element.134), channel_id=1, source_target_pairs={{2,0},{3,1},{6,4},{7,5},{10,8},{11,9},{14,12},{15,13},{18,16},{19,... | collective-permute-start | bytes 196616 | tf_op jit(solution)/shard_map/ppermute | solution.py:24
  101.3 22.0 %collective-permute-start.22 = (f32[2,1,32,256]{3,2,1,0:T(8,128)S(1)}, f32[2,1,32,256]{3,2,1,0:T(8,128)S(1)}, u32[]{:S(2)}, u32[]{:S(2)}) collective-permute-start(f32[2,1,32,256]{3,2,1,0:T(8,128)S(1)} %get-tuple-element.133), channel_id=1, source_target_pairs={{0,2},{1,3},{4,6},{5,7},{8,10},{9,11},{12,14},{13,15},{16,18},{17,... | collective-permute-start | bytes 196616 | tf_op jit(solution)/shard_map/ppermute | solution.py:22
  107.2 4.9 %collective-permute-start.27 = (f32[4,1,256]{2,0,1:T(4,128)S(1)}, f32[4,1,256]{2,0,1:T(4,128)S(1)}, u32[]{:S(2)}, u32[]{:S(2)}) collective-permute-start(f32[4,1,256]{2,0,1:T(4,128)S(1)} %collective-permute-done.25), channel_id=1, source_target_pairs={{0,1},{1,4},{4,5},{5,8},{8,9},{9,12},{12,13},{13,0},{2,3},{3,6},{6... | collective-permute-start | bytes 12296 | tf_op jit(solution)/shard_map/ppermute | solution.py:49
  107.3 4.8 %collective-permute-start.28 = (f32[4,1,256]{2,0,1:T(4,128)S(1)}, f32[4,1,256]{2,0,1:T(4,128)S(1)}, u32[]{:S(2)}, u32[]{:S(2)}) collective-permute-start(f32[4,1,256]{2,0,1:T(4,128)S(1)} %collective-permute-done.26), channel_id=1, source_target_pairs={{0,13},{1,0},{4,1},{5,4},{8,5},{9,8},{12,9},{13,12},{2,15},{3,2},{... | collective-permute-start | bytes 12296 | tf_op jit(solution)/shard_map/ppermute | solution.py:54
  112.0 4.8 %collective-permute-start.29 = (f32[4,1,256]{2,0,1:T(4,128)S(1)}, f32[4,1,256]{2,0,1:T(4,128)S(1)}, u32[]{:S(2)}, u32[]{:S(2)}) collective-permute-start(f32[4,1,256]{2,0,1:T(4,128)S(1)} %collective-permute-done.27), channel_id=1, source_target_pairs={{0,1},{1,4},{4,5},{5,8},{8,9},{9,12},{12,13},{13,0},{2,3},{3,6},{6... | collective-permute-start | bytes 12296 | tf_op jit(solution)/shard_map/ppermute | solution.py:49
  112.1 4.8 %collective-permute-start.30 = (f32[4,1,256]{2,0,1:T(4,128)S(1)}, f32[4,1,256]{2,0,1:T(4,128)S(1)}, u32[]{:S(2)}, u32[]{:S(2)}) collective-permute-start(f32[4,1,256]{2,0,1:T(4,128)S(1)} %collective-permute-done.28), channel_id=1, source_target_pairs={{0,13},{1,0},{4,1},{5,4},{8,5},{9,8},{12,9},{13,12},{2,15},{3,2},{... | collective-permute-start | bytes 12296 | tf_op jit(solution)/shard_map/ppermute | solution.py:54
  116.9 4.8 %collective-permute-start.31 = (f32[4,1,256]{2,0,1:T(4,128)S(1)}, f32[4,1,256]{2,0,1:T(4,128)S(1)}, u32[]{:S(2)}, u32[]{:S(2)}) collective-permute-start(f32[4,1,256]{2,0,1:T(4,128)S(1)} %collective-permute-done.29), channel_id=1, source_target_pairs={{0,1},{1,4},{4,5},{5,8},{8,9},{9,12},{12,13},{13,0},{2,3},{3,6},{6... | collective-permute-start | bytes 12296 | tf_op jit(solution)/shard_map/ppermute | solution.py:49
  123.6 61.7 %collective-permute-start.32 = (f32[2,6,1,256]{3,1,2,0:T(8,128)S(1)}, f32[2,6,1,256]{3,1,2,0:T(8,128)S(1)}, u32[]{:S(2)}, u32[]{:S(2)}) collective-permute-start(f32[2,6,1,256]{3,1,2,0:T(8,128)S(1)} %slice.192), channel_id=1, source_target_pairs={{0,1},{2,3},{4,5},{6,7},{8,9},{10,11},{12,13},{14,15},{16,17},{18,... | collective-permute-start | bytes 36872 | tf_op jit(solution)/shard_map/ppermute | solution.py:22
  125.8 13.8 %collective-permute-start.24 = (f32[2,6,1,256]{1,3,2,0:T(8,128)}, f32[2,6,1,256]{1,3,2,0:T(8,128)}, u32[]{:S(2)}, u32[]{:S(2)}) collective-permute-start(f32[2,6,1,256]{1,3,2,0:T(8,128)} %copy.292), channel_id=1, source_target_pairs={{1,0},{3,2},{5,4},{7,6},{9,8},{11,10},{13,12},{15,14},{17,16},{19,... | collective-permute-start | bytes 36872 | tf_op jit(solution)/shard_map/ppermute | solution.py:24
  136.2 40.4 %all-to-all-start.2 = ((f32[4,1,8192]{2,1,0:T(1,128)}), f32[4,1,8192]{2,1,0:T(1,128)S(1)}, u32[]{:S(2)}, u32[]{:S(2)}) async-start(f32[4,1,8192]{2,1,0:T(1,128)} %reshape.118), calls=%async_computation.2 | async-start | bytes 262144 | tf_op jit(solution)/shard_map/all_to_all | solution.py:162
  183.5 1.9 copy-start.9
  188.5 15.1 %collective-permute-start.36 = (f32[4,1,256]{2,0,1:T(4,128)S(1)}, f32[4,1,256]{2,0,1:T(4,128)S(1)}, u32[]{:S(2)}, u32[]{:S(2)}) collective-permute-start(f32[4,1,256]{2,0,1:T(4,128)S(1)} %get-tuple-element.143), channel_id=1, source_target_pairs={{0,1},{1,4},{4,5},{5,8},{8,9},{9,12},{12,13},{13,0},{2,3},{3,6},{6... | collective-permute-start | bytes 12296 | tf_op jit(solution)/shard_map/ppermute | solution.py:49
  188.5 15.2 %collective-permute-start.37 = (f32[4,1,256]{2,0,1:T(4,128)S(1)}, f32[4,1,256]{2,0,1:T(4,128)S(1)}, u32[]{:S(2)}, u32[]{:S(2)}) collective-permute-start(f32[4,1,256]{2,0,1:T(4,128)S(1)} %get-tuple-element.143), channel_id=1, source_target_pairs={{0,13},{1,0},{4,1},{5,4},{8,5},{9,8},{12,9},{13,12},{2,15},{3,2},{... | collective-permute-start | bytes 12296 | tf_op jit(solution)/shard_map/ppermute | solution.py:54
  192.1 37.0 %all-to-all-start.3 = ((f32[4,32,256]{2,0,1:T(4,128)}), f32[4,32,256]{2,0,1:T(4,128)S(1)}, u32[]{:S(2)}, u32[]{:S(2)}) async-start(f32[4,32,256]{2,0,1:T(4,128)} %multiply_subtract_fusion.1), calls=%async_computation.3 | async-start | bytes 262144 | tf_op jit(solution)/shard_map/all_to_all | solution.py:180
  195.4 29.9 %copy-start.6 = (f32[4,32,256]{2,1,0:T(8,128)S(1)}, f32[4,32,256]{2,1,0:T(8,128)}, u32[]{:S(2)}) copy-start(f32[4,32,256]{2,1,0:T(8,128)} %param.20) | copy-start | bytes 393220
  196.4 22.7 %collective-permute-start.34 = (f32[2,1,32,256]{3,2,1,0:T(8,128)S(1)}, f32[2,1,32,256]{3,2,1,0:T(8,128)S(1)}, u32[]{:S(2)}, u32[]{:S(2)}) collective-permute-start(f32[2,1,32,256]{3,2,1,0:T(8,128)S(1)} %get-tuple-element.130), channel_id=1, source_target_pairs={{2,0},{3,1},{6,4},{7,5},{10,8},{11,9},{14,12},{15,13},{18,16},{19,... | collective-permute-start | bytes 196616 | tf_op jit(solution)/shard_map/ppermute | solution.py:24
  197.7 21.4 %collective-permute-start.33 = (f32[2,1,32,256]{3,2,1,0:T(8,128)S(1)}, f32[2,1,32,256]{3,2,1,0:T(8,128)S(1)}, u32[]{:S(2)}, u32[]{:S(2)}) collective-permute-start(f32[2,1,32,256]{3,2,1,0:T(8,128)S(1)} %get-tuple-element.129), channel_id=1, source_target_pairs={{0,2},{1,3},{4,6},{5,7},{8,10},{9,11},{12,14},{13,15},{16,18},{17,... | collective-permute-start | bytes 196616 | tf_op jit(solution)/shard_map/ppermute | solution.py:22
  203.6 4.9 %collective-permute-start.38 = (f32[4,1,256]{2,0,1:T(4,128)S(1)}, f32[4,1,256]{2,0,1:T(4,128)S(1)}, u32[]{:S(2)}, u32[]{:S(2)}) collective-permute-start(f32[4,1,256]{2,0,1:T(4,128)S(1)} %collective-permute-done.36), channel_id=1, source_target_pairs={{0,1},{1,4},{4,5},{5,8},{8,9},{9,12},{12,13},{13,0},{2,3},{3,6},{6... | collective-permute-start | bytes 12296 | tf_op jit(solution)/shard_map/ppermute | solution.py:49
  203.7 4.8 %collective-permute-start.39 = (f32[4,1,256]{2,0,1:T(4,128)S(1)}, f32[4,1,256]{2,0,1:T(4,128)S(1)}, u32[]{:S(2)}, u32[]{:S(2)}) collective-permute-start(f32[4,1,256]{2,0,1:T(4,128)S(1)} %collective-permute-done.37), channel_id=1, source_target_pairs={{0,13},{1,0},{4,1},{5,4},{8,5},{9,8},{12,9},{13,12},{2,15},{3,2},{... | collective-permute-start | bytes 12296 | tf_op jit(solution)/shard_map/ppermute | solution.py:54
  208.5 4.8 %collective-permute-start.40 = (f32[4,1,256]{2,0,1:T(4,128)S(1)}, f32[4,1,256]{2,0,1:T(4,128)S(1)}, u32[]{:S(2)}, u32[]{:S(2)}) collective-permute-start(f32[4,1,256]{2,0,1:T(4,128)S(1)} %collective-permute-done.38), channel_id=1, source_target_pairs={{0,1},{1,4},{4,5},{5,8},{8,9},{9,12},{12,13},{13,0},{2,3},{3,6},{6... | collective-permute-start | bytes 12296 | tf_op jit(solution)/shard_map/ppermute | solution.py:49
  208.5 4.8 %collective-permute-start.41 = (f32[4,1,256]{2,0,1:T(4,128)S(1)}, f32[4,1,256]{2,0,1:T(4,128)S(1)}, u32[]{:S(2)}, u32[]{:S(2)}) collective-permute-start(f32[4,1,256]{2,0,1:T(4,128)S(1)} %collective-permute-done.39), channel_id=1, source_target_pairs={{0,13},{1,0},{4,1},{5,4},{8,5},{9,8},{12,9},{13,12},{2,15},{3,2},{... | collective-permute-start | bytes 12296 | tf_op jit(solution)/shard_map/ppermute | solution.py:54
  213.3 4.8 %collective-permute-start.42 = (f32[4,1,256]{2,0,1:T(4,128)S(1)}, f32[4,1,256]{2,0,1:T(4,128)S(1)}, u32[]{:S(2)}, u32[]{:S(2)}) collective-permute-start(f32[4,1,256]{2,0,1:T(4,128)S(1)} %collective-permute-done.40), channel_id=1, source_target_pairs={{0,1},{1,4},{4,5},{5,8},{8,9},{9,12},{12,13},{13,0},{2,3},{3,6},{6... | collective-permute-start | bytes 12296 | tf_op jit(solution)/shard_map/ppermute | solution.py:49
  219.5 5.8 %collective-permute-start.43 = (f32[2,6,1,256]{3,1,2,0:T(8,128)S(1)}, f32[2,6,1,256]{3,1,2,0:T(8,128)S(1)}, u32[]{:S(2)}, u32[]{:S(2)}) collective-permute-start(f32[2,6,1,256]{3,1,2,0:T(8,128)S(1)} %slice.200), channel_id=1, source_target_pairs={{1,0},{3,2},{5,4},{7,6},{9,8},{11,10},{13,12},{15,14},{17,16},{19,... | collective-permute-start | bytes 36872 | tf_op jit(solution)/shard_map/ppermute | solution.py:24
  220.9 4.2 %collective-permute-start.35 = (f32[2,6,1,256]{1,3,2,0:T(8,128)S(1)}, f32[2,6,1,256]{1,3,2,0:T(8,128)S(1)}, u32[]{:S(2)}, u32[]{:S(2)}) collective-permute-start(f32[2,6,1,256]{1,3,2,0:T(8,128)S(1)} %copy.295), channel_id=1, source_target_pairs={{0,1},{2,3},{4,5},{6,7},{8,9},{10,11},{12,13},{14,15},{16,17},{18,... | collective-permute-start | bytes 36872 | tf_op jit(solution)/shard_map/ppermute | solution.py:22
